TPU v7x, 256 devices: a whole 4x4x8 slice. The times are simulated.
256 devices in a mesh: seq: 16 (over y, x), head: 8 (over z), dp: 2 (over core).
Axes of the slice: x: 4, y: 4, z: 8, core: 2. Of those that a mesh axis runs over, the one named last changes fastest.
Arguments:
- hidden: bfloat16 [8192, 2560], P(('dp', 'seq', 'head')), parts along dimension 0, may hold values from -6 to 6
- x_input: bfloat16 [8192, 5120], P(('dp', 'seq', 'head')), parts along dimension 0, may hold values from -6 to 6
- grad_out: bfloat16 [8192, 5120], P(('dp', 'seq', 'head')), parts along dimension 0, may hold values from -6 to 6
- bc_weight: bfloat16 [2560, 256], replicated, may hold values from -0.01953125 to 0.01953125
- dt_weight: bfloat16 [2560, 80], replicated, may hold values from -0.125 to 0.125
- dt_bias: float32 [80], replicated, may hold values from -3 to -2
- a_log: float32 [80], replicated, may hold values from -10 to -1.6
- d_skip: float32 [80], replicated, may hold values from 0.5 to 1.5
Outputs:
- mixer_out: bfloat16 [8192, 5120], P(('dp', 'seq', 'head')), parts along dimension 0
- grad_x: bfloat16 [8192, 5120], P(('dp', 'seq', 'head')), parts along dimension 0
- grad_hidden: bfloat16 [8192, 2560], P(('dp', 'seq', 'head')), parts along dimension 0
- grad_bc_weight: float32 [5120, 256], P('dp'), parts along dimension 0
- grad_dt_weight: float32 [5120, 80], P('dp'), parts along dimension 0
- param_grads: float32 [6, 80], P('dp'), parts along dimension 0
There are 2 independent parts, one for each index of `dp`. A program takes and returns all parts, laid end to end along the dimension named above; an argument that names none is the same for every part. Nothing has to cross between parts.
All inputs are finite; a program needn't handle non-finite values.
Results may differ from a plain program's by a relative error of at most 0.02.
Values may be sent and summed in bfloat16 or wider, within the bound.
No kernel may reach another device: no remote copies, remote signals or barrier semaphores. Data moves between devices by JAX's collectives and lax.ppermute only.
A program may use at most 128 MiB of HBM per device.

v0:
```python
import jax
import jax.numpy as jnp
from jax import lax
from jax.sharding import PartitionSpec as P

Q = 256
precise = lax.Precision.HIGHEST


def prefix_2(value, axis, combine, identity):
    devices, place = (lax.axis_size(axis), lax.axis_index(axis))
    everything = jax.tree.map(
        lambda part, kind: lax.all_gather(part.astype(kind), axis),
        value,
        (jnp.bfloat16, jnp.bfloat16),
    )
    start = jax.tree.map(
        lambda part, zero: jnp.broadcast_to(jnp.asarray(zero, part.dtype), part.shape),
        value,
        identity,
    )

    def step(k, before):
        reached = k < place
        new = combine(
            before, jax.tree.map(lambda part, own: part[k].astype(own.dtype), everything, value)
        )
        return jax.tree.map(lambda a, b: jnp.where(reached, a, b), new, before)

    return lax.fori_loop(0, devices, step, start)


def prefix_3(part, axis, combine, identity):
    count = lax.axis_size(axis)
    place = lax.axis_index(axis)
    ahead = count - 1 - place
    gathered = jax.tree.map(lambda a: lax.all_gather(a, axis), part)
    state = jax.tree.map(lambda a, e: jnp.zeros_like(a) + jnp.asarray(e, a.dtype), part, identity)

    def one(step, state):
        source = count - 1 - step
        return combine(
            state, jax.tree.map(lambda a: lax.dynamic_index_in_dim(a, source, 0, False), gathered)
        )

    return lax.fori_loop(0, ahead, one, state)


def span_scan(x_heads, step_size, b_rows, c_rows, neg_rate, state_in):
    length = x_heads.shape[0]
    blocks = length // Q
    heads_here = x_heads.shape[1]
    head_width = x_heads.shape[2]
    states = b_rows.shape[1]
    causal = (jnp.arange(Q)[:, None] >= jnp.arange(Q)[None, :])[:, :, None]

    def span_advance(carry, block):
        x_block, step_block, b_block, c_block = block
        running = jnp.cumsum(step_block * neg_rate[None, :], axis=0)
        scores = jnp.dot(c_block, b_block.T, precision=precise)
        spread = running[:, None, :] - running[None, :, :]
        decay = jnp.where(causal, jnp.exp(jnp.where(causal, spread, 0.0)), 0.0)
        scaled_x = x_block * step_block[:, :, None]
        inner = jnp.einsum("qkh,khp->qhp", decay * scores[:, :, None], scaled_x, precision=precise)
        carried = (
            jnp.einsum("qn,hnp->qhp", c_block, carry, precision=precise)
            * jnp.exp(running)[:, :, None]
        )
        total = running[-1]
        weights_end = jnp.exp(total[None, :] - running)
        fresh = jnp.einsum(
            "kn,khp->hnp", b_block, scaled_x * weights_end[:, :, None], precision=precise
        )
        return (jnp.exp(total)[:, None, None] * carry + fresh, inner + carried)

    pieces = (
        x_heads.reshape(blocks, Q, heads_here, head_width),
        step_size.reshape(blocks, Q, heads_here),
        b_rows.reshape(blocks, Q, states),
        c_rows.reshape(blocks, Q, states),
    )
    state_out, outputs = lax.scan(jax.checkpoint(span_advance), state_in, pieces)
    return (outputs.reshape(length, heads_here, head_width), state_out)


def mixer_local(x_heads, raw_step, b_rows, c_rows, log_decay, skip_gain, step_bias, state_in):
    step_size = jax.nn.softplus(raw_step + step_bias[None, :])
    neg_rate = -jnp.exp(log_decay)
    mixed, state_out = span_scan(x_heads, step_size, b_rows, c_rows, neg_rate, state_in)
    return (mixed + skip_gain[None, :, None] * x_heads, state_out)


def device_totals(x_heads, step_size, b_rows, c_rows, grad_heads, neg_rate):
    length = x_heads.shape[0]
    heads_here = x_heads.shape[1]
    head_width = x_heads.shape[2]
    states = b_rows.shape[1]
    blocks = length // Q

    def device_advance(carry, block):
        prefix, state_sum, adjoint_sum = carry
        x_block, step_block, b_block, c_block, grad_block = block
        running = jnp.cumsum(step_block * neg_rate[None, :], axis=0)
        total = running[-1]
        weights_end = jnp.exp(total[None, :] - running)
        scaled_x = x_block * step_block[:, :, None]
        fresh = jnp.einsum(
            "kn,khp->hnp", b_block, scaled_x * weights_end[:, :, None], precision=precise
        )
        state_sum = jnp.exp(total)[:, None, None] * state_sum + fresh
        reach = jnp.exp(prefix[None, :] + running)
        adjoint_sum = adjoint_sum + jnp.einsum(
            "qn,qhp->hnp", c_block, grad_block * reach[:, :, None], precision=precise
        )
        return ((prefix + total, state_sum, adjoint_sum), None)

    pieces = (
        x_heads.reshape(blocks, Q, heads_here, head_width),
        step_size.reshape(blocks, Q, heads_here),
        b_rows.reshape(blocks, Q, states),
        c_rows.reshape(blocks, Q, states),
        grad_heads.reshape(blocks, Q, heads_here, head_width),
    )
    start = (
        jnp.zeros((heads_here,), jnp.float32),
        jnp.zeros((heads_here, states, head_width), jnp.float32),
        jnp.zeros((heads_here, states, head_width), jnp.float32),
    )
    (prefix, state_sum, adjoint_sum), unused = lax.scan(device_advance, start, pieces)
    return (jnp.exp(prefix), state_sum, adjoint_sum)


def combine_pairs(earlier, later):
    return (earlier[0] * later[0], later[0][:, None, None] * earlier[1] + later[1])


def per_device(hidden, x_input, grad_out, bc_weight, dt_weight, dt_bias, a_log, d_skip):
    groups = lax.axis_size("head")
    head_index = lax.axis_index("head")
    heads_all = dt_weight.shape[1]
    heads_local = heads_all // groups
    head_width = x_input.shape[1] // heads_all
    states = bc_weight.shape[1] // 2
    proj_bc = jnp.dot(hidden, bc_weight, preferred_element_type=jnp.float32).astype(jnp.bfloat16)
    proj_dt = jnp.dot(hidden, dt_weight, preferred_element_type=jnp.float32).astype(jnp.bfloat16)
    x_local, raw_local, grad_local = (
        lax.all_to_all(x_input, "head", split_axis=1, concat_axis=0, tiled=True),
        lax.all_to_all(proj_dt, "head", split_axis=1, concat_axis=0, tiled=True),
        lax.all_to_all(grad_out, "head", split_axis=1, concat_axis=0, tiled=True),
    )
    bc_local = lax.all_gather(proj_bc, "head", axis=0, tiled=True)
    length = x_local.shape[0]
    x_heads = x_local.astype(jnp.float32).reshape(length, heads_local, head_width)
    grad_heads = grad_local.astype(jnp.float32).reshape(length, heads_local, head_width)
    raw_step = raw_local.astype(jnp.float32)
    b_rows = bc_local[:, :states].astype(jnp.float32)
    c_rows = bc_local[:, states:].astype(jnp.float32)
    offset = head_index * heads_local
    bias_local = lax.dynamic_slice_in_dim(dt_bias, offset, heads_local)
    log_local = lax.dynamic_slice_in_dim(a_log, offset, heads_local)
    skip_local = lax.dynamic_slice_in_dim(d_skip, offset, heads_local)
    step_size = jax.nn.softplus(raw_step + bias_local[None, :])
    neg_rate = -jnp.exp(log_local)
    decay_all, state_sum, adjoint_sum = device_totals(
        x_heads, step_size, b_rows, c_rows, grad_heads, neg_rate
    )
    identity = (
        jnp.ones((heads_local,), jnp.float32),
        jnp.zeros((heads_local, states, head_width), jnp.float32),
    )
    state_in = prefix_2((decay_all, state_sum), "seq", combine_pairs, identity)[1]
    state_grad = prefix_3((decay_all, adjoint_sum), "seq", combine_pairs, identity)[1]

    def forward(x_arg, raw_arg, b_arg, c_arg, log_arg, skip_arg, bias_arg):
        return mixer_local(x_arg, raw_arg, b_arg, c_arg, log_arg, skip_arg, bias_arg, state_in)

    (mixed, state_end), pullback = jax.vjp(
        forward, x_heads, raw_step, b_rows, c_rows, log_local, skip_local, bias_local
    )
    grad_xs, grad_raw, grad_b, grad_c, grad_alog, grad_skip, grad_bias = pullback(
        (grad_heads, state_grad)
    )
    out_local = mixed.reshape(length, heads_local * head_width).astype(jnp.bfloat16)
    gradx_local = grad_xs.reshape(length, heads_local * head_width).astype(jnp.bfloat16)
    step_local = grad_raw.astype(jnp.bfloat16)
    mixer_out, grad_x, d_step = (
        lax.all_to_all(out_local, "head", split_axis=0, concat_axis=1, tiled=True),
        lax.all_to_all(gradx_local, "head", split_axis=0, concat_axis=1, tiled=True),
        lax.all_to_all(step_local, "head", split_axis=0, concat_axis=1, tiled=True),
    )
    d_bc = lax.psum_scatter(
        jnp.concatenate([grad_b, grad_c], axis=1).astype(jnp.bfloat16),
        "head",
        scatter_dimension=0,
        tiled=True,
    )
    grad_hidden = (
        jnp.dot(d_bc, bc_weight.T, preferred_element_type=jnp.float32)
        + jnp.dot(d_step, dt_weight.T, preferred_element_type=jnp.float32)
    ).astype(jnp.bfloat16)
    seq_total = length * lax.axis_size("seq")
    weight_bc = jnp.dot(hidden.T, d_bc, preferred_element_type=jnp.float32) / seq_total
    weight_dt = jnp.dot(hidden.T, d_step, preferred_element_type=jnp.float32) / seq_total
    stacked = jnp.stack([grad_bias, grad_alog, grad_skip]) / seq_total
    param_local = lax.dynamic_update_slice(
        jnp.zeros((3, heads_all), jnp.float32), stacked, (0, offset)
    )
    grad_bc_weight, grad_dt_weight, param_grads = lax.psum(
        (weight_bc, weight_dt, param_local), ("seq", "head")
    )
    return (mixer_out, grad_x, grad_hidden, grad_bc_weight, grad_dt_weight, param_grads)


def solution(mesh):
    in_specs = (
        P(("dp", "seq", "head"), None),
        P(("dp", "seq", "head"), None),
        P(("dp", "seq", "head"), None),
        P(),
        P(),
        P(),
        P(),
        P(),
    )
    out_specs = (
        P(("dp", "seq", "head"), None),
        P(("dp", "seq", "head"), None),
        P(("dp", "seq", "head"), None),
        P("dp", None),
        P("dp", None),
        P("dp", None),
    )
    return jax.shard_map(
        per_device, mesh=mesh, in_specs=in_specs, out_specs=out_specs, check_vma=False
    )
```

profile of v0, /device:TPU:0, one launch (start us, length us, event | category | flops | bytes accessed | tf_op | source)
XLA Modules:
  0.0 757.0 jit_solution(9546356608684292287)
XLA Ops:
  9.5 6.7 all-to-all-start.1
  19.9 4.0 all-to-all-done.1
  23.9 3.4 all-to-all-start
  27.4 27.6 %all_gather.23 = bf16[256,256]{1,0:T(8,128)(2,1)S(1)} all-gather(bf16[32,256]{1,0:T(8,128)(2,1)S(1)} %convolution_convert_fusion), channel_id=1, replica_groups=mesh['seq'=16,'head'=8,'dp'=2] {'head'}, dimensions={0}, use_global_device_ids=true | all-gather | bytes 147456 | tf_op jit(solution)/shard_map/all_gather | solution.py:151
  57.0 6.1 all-to-all-start.3
  77.8 3.5 multiply_reduce_fusion
  91.4 20.9 %all-gather.2 = bf16[16,1,10]{2,1,0:T(2,128)(2,1)S(1)} all-gather(bf16[1,1,10]{2,1,0:T(2,128)(2,1)S(1)} %bitcast.278), channel_id=1, replica_groups=mesh['seq'=16,'head'=8,'dp'=2] {'seq'}, dimensions={0}, use_global_device_ids=true | all-gather | bytes 340 | tf_op jit(solution)/shard_map/all_gather | solution.py:13
  112.3 21.2 %all-gather.3 = f32[16,1,10]{2,1,0:T(1,128)} all-gather(f32[1,1,10]{2,1,0:T(1,128)} %bitcast.276), channel_id=1, replica_groups=mesh['seq'=16,'head'=8,'dp'=2] {'seq'}, dimensions={0}, use_global_device_ids=true | all-gather | bytes 680 | tf_op jit(solution)/shard_map/all_gather | solution.py:37
  139.1 22.0 %while.21 = (s32[]{:T(128)}, f32[10,128,64]{2,1,0:T(8,128)S(1)}, s32[]{:T(128)}, bf16[16,10]{1,0:T(8,128)(2,1)S(1)}, bf16[16,10,128,64]{2,3,1,0:T(8,128)(2,1)}, /*index=5*/s32[]{:T(128)}, s32[]{:T(128)}) while((s32[]{:T(128)}, f32[10,128,64]{2,1,0:T(8,128)S(1)}, s32[]{:T(128)}, bf16[16,10]{1,0:T(8,128)(2,1)S(1)}, ...), condition=%wide.region_3.4_spmd.clone, body=%wide.region_2.3_spmd.clone.sunk | while | flops 409614 | bytes 1474765 | solution.py:30
  161.1 41.3 %all-gather.9.cloned.1.call-done = f32[160,128,64]{1,2,0:T(8,128)} async-done(((f32[10,128,64]{1,2,0:T(8,128)}), f32[160,128,64]{1,2,0:T(8,128)}) %all-gather.9.cloned.1.call-update) | async-done | bytes 5242896 | tf_op jit(solution)/shard_map/all_gather | solution.py:37
  202.5 57.5 %while.20 = (s32[]{:T(128)}, f32[10,128,64]{2,1,0:T(8,128)S(1)}, s32[]{:T(128)}, f32[16,10]{1,0:T(8,128)}, f32[16,10,128,64]{2,3,1,0:T(8,128)}, /*index=5*/s32[]{:T(128)}, s32[]{:T(128)}, s32[]{:T(128)}, s32[]{:T(128)}) while((s32[]{:T(128)}, f32[10,128,64]{2,1,0:T(8,128)S(1)}, s32[]{:T(128)}, f32[16,10]{1,0:T(8,128)}, ...), condition=%wide.region_5.6_spmd, body=%wide.region_4.5_spmd.sunk | while | flops 163846 | bytes 2294027 | solution.py:46
  268.0 3.0 copy.262
  278.4 5.8 fusion.19
  284.3 3.9 multiply_reduce_fusion.3
  302.8 7.0 all-to-all-start.5
  310.7 6.8 all-to-all-done.5
  318.8 28.1 %reduce-scatter.4.cloned.1.call-done = bf16[32,256]{1,0:T(8,128)(2,1)} async-done(((bf16[256,256]{1,0:T(8,128)(2,1)}), bf16[32,256]{1,0:T(8,128)(2,1)}) %reduce-scatter.4.cloned.1.call-update) | async-done | bytes 16400
  350.5 3.6 broadcast_multiply_fusion.1
  354.8 6.0 fusion.48
  370.9 4.4 all-to-all-start.2
  375.6 14.4 %all-to-all-done.2 = bf16[8,32,640]{2,1,0:T(8,128)(2,1)S(1)} async-done(((bf16[8,32,640]{2,1,0:T(8,128)(2,1)}), bf16[8,32,640]{2,1,0:T(8,128)(2,1)S(1)}, u32[]{:S(2)}, u32[]{:S(2)}) %all-to-all-start.2) | async-done | bytes 327712 | tf_op jit(solution)/shard_map/all_to_all | solution.py:187
  390.0 3.4 all-to-all-start.4
  393.6 349.3 %psum.23 = f32[3,80]{1,0:T(4,128)} all-reduce(f32[3,80]{1,0:T(4,128)S(1)} %dynamic_update_slice.19), channel_id=1, replica_groups=mesh['seq'=16,'head'=8,'dp'=2] {'seq','head'}, use_global_device_ids=true, to_apply=%region_25.26 | all-reduce | flops 240 | bytes 1920 | tf_op jit(solution)/shard_map/psum | solution.py:208
  745.9 3.3 copy.269
  (357 shorter events, 166.7 us)
Async XLA Ops:
  7.2 9.0 %copy-start = (bf16[2560,256]{1,0:T(8,128)(2,1)S(1)}, bf16[2560,256]{1,0:T(8,128)(2,1)}, u32[]{:S(2)}) copy-start(bf16[2560,256]{1,0:T(8,128)(2,1)} %param.15) | copy-start | bytes 3932164
  7.2 47.8 %copy-start.45 = (f32[80]{0:T(128)S(1)}, f32[80]{0:T(128)}, u32[]{:S(2)}) copy-start(f32[80]{0:T(128)} %param.17) | copy-start | bytes 964
  7.2 47.9 %copy-start.14 = (bf16[32,5120]{1,0:T(8,128)(2,1)S(1)}, bf16[32,5120]{1,0:T(8,128)(2,1)}, u32[]{:S(2)}) copy-start(bf16[32,5120]{1,0:T(8,128)(2,1)} %param.14) | copy-start | bytes 983044
  9.5 14.5 %all-to-all-start.1 = ((bf16[8,2,160]{2,1,0:T(2,128)(2,1)}), bf16[8,2,160]{2,1,0:T(2,128)(2,1)S(1)}, u32[]{:S(2)}, u32[]{:S(2)}) async-start(bf16[8,2,160]{2,1,0:T(2,128)(2,1)} %reshape.399), calls=%async_computation.1 | async-start | bytes 16384 | tf_op jit(solution)/shard_map/all_to_all | solution.py:148
  18.2 46.4 %copy-start.34 = (f32[10]{0:T(128)}, f32[10]{0:T(128)S(1)}, u32[]{:S(2)}) copy-start(f32[10]{0:T(128)S(1)} %fusion.113) | copy-start | bytes 124
  23.9 33.0 %all-to-all-start = ((bf16[32,8,640]{2,0,1:T(8,128)(2,1)}), bf16[32,8,640]{2,0,1:T(8,128)(2,1)S(1)}, u32[]{:S(2)}, u32[]{:S(2)}) async-start(bf16[32,8,640]{2,0,1:T(8,128)(2,1)} %bitcast.236), calls=%async_computation | async-start | bytes 655360 | tf_op jit(solution)/shard_map/all_to_all | solution.py:147
  55.1 9.6 %copy-start.36 = (f32[10]{0:T(128)}, f32[10]{0:T(128)S(1)}, u32[]{:S(2)}) copy-start(f32[10]{0:T(128)S(1)} %dynamic_slice.73) | copy-start | bytes 124
  57.0 20.9 %all-to-all-start.3 = ((bf16[32,8,640]{2,0,1:T(8,128)(2,1)}), bf16[32,8,640]{2,0,1:T(8,128)(2,1)}, u32[]{:S(2)}, u32[]{:S(2)}) async-start(bf16[32,8,640]{2,0,1:T(8,128)(2,1)} %bitcast.235), calls=%async_computation.3 | async-start | bytes 655360 | tf_op jit(solution)/shard_map/all_to_all | solution.py:149
  63.0 76.1 %all-gather.7.cloned.1.call-start = ((), (), s32[]{:S(2)}) async-start(), calls=%async_computation.7 | async-start | bytes 2785280 | tf_op jit(solution)/shard_map/all_gather | solution.py:13
  85.5 117.0 %all-gather.9.cloned.1.call-start = ((), (), s32[]{:S(2)}) async-start(), calls=%async_computation.8 | async-start | bytes 5570560 | tf_op jit(solution)/shard_map/all_gather | solution.py:37
  90.5 176.4 %copy-start.3 = (f32[256,128]{1,0:T(8,128)}, f32[256,128]{1,0:T(8,128)S(1)}, u32[]{:S(2)}) copy-start(f32[256,128]{1,0:T(8,128)S(1)} %get-tuple-element.368) | copy-start | bytes 393220
  261.7 9.3 %copy-start.38 = (f32[10]{0:T(128)}, f32[10]{0:T(128)S(1)}, u32[]{:S(2)}) copy-start(f32[10]{0:T(128)S(1)} %slice_bitcast_fusion) | copy-start | bytes 124
  298.5 19.2 %copy-start.2 = (bf16[32,2560]{1,0:T(8,128)(2,1)S(1)}, bf16[32,2560]{1,0:T(8,128)(2,1)}, u32[]{:S(2)}) copy-start(bf16[32,2560]{1,0:T(8,128)(2,1)} %param.12) | copy-start | bytes 491524
  302.8 14.7 %all-to-all-start.5 = ((bf16[8,2,160]{2,1,0:T(2,128)(2,1)}), bf16[8,2,160]{2,1,0:T(2,128)(2,1)S(1)}, u32[]{:S(2)}, u32[]{:S(2)}) async-start(bf16[8,2,160]{2,1,0:T(2,128)(2,1)} %reshape.401), calls=%async_computation.5 | async-start | bytes 16384 | tf_op jit(solution)/shard_map/all_to_all | solution.py:189
  309.8 37.1 %reduce-scatter.4.cloned.1.call-start = ((), (), s32[]{:S(2)}) async-start(), calls=%async_computation.9 | async-start | bytes 147456
  310.7 435.2 %all-reduce.4.cloned.1.call-start = ((), (), s32[]{:S(2)}) async-start(), calls=%async_computation.10 | async-start | bytes 6881280 | tf_op jit(solution)/shard_map/psum | solution.py:208
  317.7 32.0 %copy-start.18 = (bf16[32,80]{0,1:T(8,128)(2,1)}, bf16[32,80]{0,1:T(8,128)(2,1)S(1)}, u32[]{:S(2)}) copy-start(bf16[32,80]{0,1:T(8,128)(2,1)S(1)} %all_to_all.80) | copy-start | bytes 15364
  318.8 30.8 %copy-start.46 = (f32[80]{0:T(128)S(1)}, f32[80]{0:T(128)}, u32[]{:S(2)}) copy-start(f32[80]{0:T(128)} %param.19) | copy-start | bytes 964
  368.3 25.2 %copy-start.40 = (f32[10]{0:T(128)S(1)}, f32[10]{0:T(128)}, u32[]{:S(2)}) copy-start(f32[10]{0:T(128)} %get-tuple-element.530) | copy-start | bytes 124
  368.3 374.6 %copy-start.24 = (bf16[32,256]{1,0:T(8,128)(2,1)S(1)}, bf16[32,256]{1,0:T(8,128)(2,1)}, u32[]{:S(2)}) copy-start(bf16[32,256]{1,0:T(8,128)(2,1)} %reduce-scatter.4.cloned.1.call-done) | copy-start | bytes 49156
  368.3 375.1 %copy-start.7 = (bf16[2560,80]{0,1:T(8,128)(2,1)S(1)}, bf16[2560,80]{0,1:T(8,128)(2,1)}, u32[]{:S(2)}) copy-start(bf16[2560,80]{0,1:T(8,128)(2,1)} %param.16) | copy-start | bytes 1228804
  368.3 375.1 %copy-start.19 = (bf16[32,80]{0,1:T(8,128)(2,1)S(1)}, bf16[32,80]{0,1:T(8,128)(2,1)}, u32[]{:S(2)}) copy-start(bf16[32,80]{0,1:T(8,128)(2,1)} %copy-done.18) | copy-start | bytes 15364
  370.9 19.1 %all-to-all-start.2 = ((bf16[8,32,640]{2,1,0:T(8,128)(2,1)}), bf16[8,32,640]{2,1,0:T(8,128)(2,1)S(1)}, u32[]{:S(2)}, u32[]{:S(2)}) async-start(bf16[8,32,640]{2,1,0:T(8,128)(2,1)} %get-tuple-element.546), calls=%async_computation.2 | async-start | bytes 655360 | tf_op jit(solution)/shard_map/all_to_all | solution.py:187
  390.0 355.1 %all-to-all-start.4 = ((bf16[8,32,640]{2,1,0:T(8,128)(2,1)}), bf16[8,32,640]{2,1,0:T(8,128)(2,1)S(1)}, u32[]{:S(2)}, u32[]{:S(2)}) async-start(bf16[8,32,640]{2,1,0:T(8,128)(2,1)} %get-tuple-element.545), calls=%async_computation.4 | async-start | bytes 655360 | tf_op jit(solution)/shard_map/all_to_all | solution.py:188
  (33 other events, 154.3 us)
Sparse Core Ops, SparseCore 0:
  85.6 52.9 all-gather.6
  141.6 60.7 all-gather.8
  313.7 33.1 reduce-scatter.3
  353.9 237.4 all-reduce.3
where the time goes:
time: 768 us; the launch traced here: 757 us
  blocking collectives  419 us (55%)
  local copies, waits for them, and re-layouts  124 us (16%)
  waiting for transfers between devices  94.7 us (12%)
  matrix products  38.5 us (5%)
  other arithmetic  32.8 us (4%)
  starting transfers between devices  31.3 us (4%)
  between operations  14.9 us (2%)
    psum x1, blocking collectives, per_device(): lax.psum((weight_bc, weight_dt, param_local), ('seq', 'head'))  349 us
    dynamic_slice x30, local copies, waits for them, and re-layouts, one(): lax.dynamic_index_in_dim(a, source, 0, False)  44 us
    all_gather x1, waiting for transfers between devices, prefix_3(): gathered = jax.tree.map(lambda a: lax.all_gather(a, axis), part)  41.3 us
    unnamed x5, waiting for transfers between devices  28.1 us
    all_gather x1, blocking collectives, per_device(): bc_local = lax.all_gather(proj_bc, 'head', axis=0, tiled=True)  27.6 us
    all_gather x1, blocking collectives, prefix_3(): gathered = jax.tree.map(lambda a: lax.all_gather(a, axis), part)  21.2 us
    all_gather x1, blocking collectives, prefix_2(): lax.all_gather(part.astype(kind), axis)  20.9 us
    dynamic_slice x32, local copies, waits for them, and re-layouts, step(): part[k].astype(own.dtype)  18.6 us
  transfers between devices with their start and end apart: 10, of which 5 were waited for; matrix products, arithmetic and copies ran while one was open for 10% of the time, Pallas kernels for 0%

commit v1 on v0

--- a/solution.py
+++ b/solution.py
@@ -206,7 +206,7 @@
         jnp.zeros((3, heads_all), jnp.float32), stacked, (0, offset)
     )
     grad_bc_weight, grad_dt_weight, param_grads = lax.psum(
-        (weight_bc, weight_dt, param_local), ("seq", "head")
+        lax.psum((weight_bc, weight_dt, param_local), "head"), "seq"
     )
     return (mixer_out, grad_x, grad_hidden, grad_bc_weight, grad_dt_weight, param_grads)
 

time: 768 us -> 582 us (0.76)
  the two profiles are of different devices: /device:TPU:0 before, /device:TPU:1 now
where the time goes in v1:
time: 582 us; the launch traced here: 571 us
  waiting for transfers between devices  208 us (36%)
  local copies, waits for them, and re-layouts  130 us (22%)
  blocking collectives  105 us (18%)
  matrix products  39.7 us (7%)
  other arithmetic  38.8 us (7%)
  starting transfers between devices  32.9 us (6%)
  between operations  14.8 us (3%)
    psum x1, waiting for transfers between devices, per_device(): lax.psum((weight_bc, weight_dt, param_local), 'head')  100 us
    dynamic_slice x30, local copies, waits for them, and re-layouts, one(): lax.dynamic_index_in_dim(a, source, 0, False)  44 us
    psum x1, blocking collectives, per_device(): lax.psum(lax.psum((weight_bc, weight_dt, param_local), 'head'), 'seq')  34 us
    all_gather x1, waiting for transfers between devices, prefix_3(): gathered = jax.tree.map(lambda a: lax.all_gather(a, axis), part)  32.1 us
    unnamed x6, waiting for transfers between devices  24.1 us
    all_gather x1, blocking collectives, per_device(): bc_local = lax.all_gather(proj_bc, 'head', axis=0, tiled=True)  22.7 us
    dynamic_slice x32, local copies, waits for them, and re-layouts, step(): part[k].astype(own.dtype)  18.6 us
    psum x1, waiting for transfers between devices, per_device(): lax.psum(lax.psum((weight_bc, weight_dt, param_local), 'head'), 'seq')  18.2 us
  transfers between devices with their start and end apart: 11, of which 8 were waited for; matrix products, arithmetic and copies ran while one was open for 16% of the time, Pallas kernels for 0%

profile of v1, /device:TPU:1, one launch (start us, length us, event | category | flops | bytes accessed | tf_op | source)
XLA Modules:
  0.0 570.7 jit_solution(15210609173691321867)
XLA Ops:
  9.5 9.0 %all-to-all-start.1 = ((bf16[8,2,160]{2,1,0:T(2,128)(2,1)}), bf16[8,2,160]{2,1,0:T(2,128)(2,1)S(1)}, u32[]{:S(2)}, u32[]{:S(2)}) async-start(bf16[8,2,160]{2,1,0:T(2,128)(2,1)} %reshape.399), calls=%async_computation.1 | async-start | bytes 16384 | tf_op jit(solution)/shard_map/all_to_all | solution.py:148
  25.1 3.8 all-to-all-start
  28.9 22.7 %all_gather.23 = bf16[256,256]{1,0:T(8,128)(2,1)S(1)} all-gather(bf16[32,256]{1,0:T(8,128)(2,1)S(1)} %convolution_convert_fusion), channel_id=1, replica_groups=mesh['seq'=16,'head'=8,'dp'=2] {'head'}, dimensions={0}, use_global_device_ids=true | all-gather | bytes 147456 | tf_op jit(solution)/shard_map/all_gather | solution.py:151
  53.5 5.8 %all-to-all-start.3 = ((bf16[32,8,640]{2,0,1:T(8,128)(2,1)}), bf16[32,8,640]{2,0,1:T(8,128)(2,1)S(1)}, u32[]{:S(2)}, u32[]{:S(2)}) async-start(bf16[32,8,640]{2,0,1:T(8,128)(2,1)} %bitcast.235), calls=%async_computation.3 | async-start | bytes 655360 | tf_op jit(solution)/shard_map/all_to_all | solution.py:149
  79.4 3.6 fusion.62
  84.8 3.6 fusion.56
  90.7 16.3 %all-gather.2 = bf16[16,1,10]{2,1,0:T(2,128)(2,1)S(1)} all-gather(bf16[1,1,10]{2,1,0:T(2,128)(2,1)S(1)} %bitcast.278), channel_id=1, replica_groups=mesh['seq'=16,'head'=8,'dp'=2] {'seq'}, dimensions={0}, use_global_device_ids=true | all-gather | bytes 340 | tf_op jit(solution)/shard_map/all_gather | solution.py:13
  107.6 16.7 %all-gather.3 = f32[16,1,10]{2,1,0:T(1,128)} all-gather(f32[1,1,10]{2,1,0:T(1,128)} %bitcast.276), channel_id=1, replica_groups=mesh['seq'=16,'head'=8,'dp'=2] {'seq'}, dimensions={0}, use_global_device_ids=true | all-gather | bytes 680 | tf_op jit(solution)/shard_map/all_gather | solution.py:37
  127.9 13.9 %all-gather.7.cloned.1.call-done = bf16[160,128,64]{1,2,0:T(8,128)(2,1)} async-done(((bf16[10,128,64]{1,2,0:T(8,128)(2,1)}), bf16[160,128,64]{1,2,0:T(8,128)(2,1)}) %all-gather.7.cloned.1.call-update) | async-done | bytes 2621456 | tf_op jit(solution)/shard_map/all_gather | solution.py:13
  141.9 32.3 %while.21 = (s32[]{:T(128)}, f32[10,128,64]{2,1,0:T(8,128)S(1)}, s32[]{:T(128)}, bf16[16,10]{1,0:T(8,128)(2,1)}, bf16[16,10,128,64]{2,3,1,0:T(8,128)(2,1)}, /*index=5*/s32[]{:T(128)}, s32[]{:T(128)}) while((s32[]{:T(128)}, f32[10,128,64]{2,1,0:T(8,128)S(1)}, s32[]{:T(128)}, bf16[16,10]{1,0:T(8,128)(2,1)}, ...), condition=%wide.region_3.4_spmd.clone, body=%wide.region_2.3_spmd.clone.sunk | while | flops 409614 | bytes 1474765 | solution.py:30
  174.2 32.1 %all-gather.9.cloned.1.call-done = f32[160,128,64]{1,2,0:T(8,128)} async-done(((f32[10,128,64]{1,2,0:T(8,128)}), f32[160,128,64]{1,2,0:T(8,128)}) %all-gather.9.cloned.1.call-update) | async-done | bytes 5242896 | tf_op jit(solution)/shard_map/all_gather | solution.py:37
  206.3 57.9 %while.20 = (s32[]{:T(128)}, f32[10,128,64]{2,1,0:T(8,128)S(1)}, s32[]{:T(128)}, f32[16,10]{1,0:T(8,128)}, f32[16,10,128,64]{2,3,1,0:T(8,128)}, /*index=5*/s32[]{:T(128)}, s32[]{:T(128)}, s32[]{:T(128)}, s32[]{:T(128)}) while((s32[]{:T(128)}, f32[10,128,64]{2,1,0:T(8,128)S(1)}, s32[]{:T(128)}, f32[16,10]{1,0:T(8,128)}, ...), condition=%wide.region_5.6_spmd, body=%wide.region_4.5_spmd.sunk | while | flops 163846 | bytes 2294027 | solution.py:46
  283.5 6.0 %fusion.19 = (f32[256,10]{0,1:T(8,128)S(1)}, f32[256,10]{0,1:T(8,128)}, f32[256,256]{1,0:T(8,128)}) fusion(f32[256,256]{1,0:T(8,128)} %fusion.116, f32[256,10]{0,1:T(8,128)S(1)} %copy.249, pred[256,256]{1,0:T(8,128)(4,1)} %bitcast.268, f32[10,64,256]{2,1,0:T(8,128)} %copy.251, f32[256,10,64]{0,2,1:T(8,128)} %copy.254, f32[256,10]{0,1:T(8,128)S(1)} %get-tuple-element.364), kind=kOutput, calls=%fused_computation.30 | convolution fusion | flops 510618624 | bytes 1941504 | tf_op jit(solution)/shard_map/transpose(jvp())/while/body/eval_jaxpr/checkpoint/qkh,khp->qhp/dot_general | solution.py:64
  289.5 3.9 multiply_reduce_fusion.3
  308.2 6.7 %all-to-all-start.5 = ((bf16[8,2,160]{2,1,0:T(2,128)(2,1)}), bf16[8,2,160]{2,1,0:T(2,128)(2,1)S(1)}, u32[]{:S(2)}, u32[]{:S(2)}) async-start(bf16[8,2,160]{2,1,0:T(2,128)(2,1)} %reshape.401), calls=%async_computation.5 | async-start | bytes 16384 | tf_op jit(solution)/shard_map/all_to_all | solution.py:189
  315.8 5.7 all-to-all-done.5
  322.8 24.0 %reduce-scatter.4.cloned.1.call-done = bf16[32,256]{1,0:T(8,128)(2,1)} async-done(((bf16[256,256]{1,0:T(8,128)(2,1)}), bf16[32,256]{1,0:T(8,128)(2,1)}) %reduce-scatter.4.cloned.1.call-update) | async-done | bytes 16400
  349.6 100.4 %all-reduce.8.cloned.1.call-done = (f32[2560,256]{0,1:T(8,128)}, f32[2560,80]{0,1:T(8,128)}) async-done(((f32[2560,256]{0,1:T(8,128)}, f32[2560,80]{0,1:T(8,128)}), (f32[2560,256]{0,1:T(8,128)}, f32[2560,80]{0,1:T(8,128)})) %all-reduce.8.cloned.1.call-update) | async-done | bytes 3440656 | tf_op jit(solution)/shard_map/psum | solution.py:209
  454.8 5.2 fusion.48
  470.5 4.0 all-to-all-start.2
  474.8 11.2 %all-to-all-done.2 = bf16[8,32,640]{2,1,0:T(8,128)(2,1)S(1)} async-done(((bf16[8,32,640]{2,1,0:T(8,128)(2,1)}), bf16[8,32,640]{2,1,0:T(8,128)(2,1)S(1)}, u32[]{:S(2)}, u32[]{:S(2)}) %all-to-all-start.2) | async-done | bytes 327712 | tf_op jit(solution)/shard_map/all_to_all | solution.py:187
  489.5 15.1 %psum.46 = f32[3,80]{1,0:T(4,128)S(1)} all-reduce(f32[3,80]{1,0:T(4,128)S(1)} %dynamic_update_slice.19), channel_id=1, replica_groups=mesh['seq'=16,'head'=8,'dp'=2] {'head'}, use_global_device_ids=true, to_apply=%region_27.28 | all-reduce | flops 240 | bytes 1920 | tf_op jit(solution)/shard_map/psum | solution.py:209
  504.7 34.0 %psum.47 = f32[3,80]{1,0:T(4,128)} all-reduce(f32[3,80]{1,0:T(4,128)S(1)} %psum.46), channel_id=1, replica_groups=mesh['seq'=16,'head'=8,'dp'=2] {'seq'}, use_global_device_ids=true, to_apply=%region_28.29 | all-reduce | flops 240 | bytes 1920 | tf_op jit(solution)/shard_map/psum | solution.py:208
  541.6 18.2 %all-reduce.6.cloned.1.call-done = (f32[2560,256]{0,1:T(8,128)}, f32[2560,80]{0,1:T(8,128)}) async-done(((f32[2560,256]{0,1:T(8,128)}, f32[2560,80]{0,1:T(8,128)}), (f32[2560,256]{0,1:T(8,128)}, f32[2560,80]{0,1:T(8,128)})) %all-reduce.6.cloned.1.call-update) | async-done | bytes 3440656 | tf_op jit(solution)/shard_map/psum | solution.py:208
  (347 shorter events, 192.6 us)
Async XLA Ops:
  7.2 11.3 %copy-start = (bf16[2560,256]{1,0:T(8,128)(2,1)S(1)}, bf16[2560,256]{1,0:T(8,128)(2,1)}, u32[]{:S(2)}) copy-start(bf16[2560,256]{1,0:T(8,128)(2,1)} %param.15) | copy-start | bytes 3932164
  7.2 44.3 %copy-start.38 = (f32[80]{0:T(128)S(1)}, f32[80]{0:T(128)}, u32[]{:S(2)}) copy-start(f32[80]{0:T(128)} %param.17) | copy-start | bytes 964
  7.2 44.4 %copy-start.18 = (bf16[32,5120]{1,0:T(8,128)(2,1)S(1)}, bf16[32,5120]{1,0:T(8,128)(2,1)}, u32[]{:S(2)}) copy-start(bf16[32,5120]{1,0:T(8,128)(2,1)} %param.14) | copy-start | bytes 983044
  9.5 15.6 %all-to-all-start.1 = ((bf16[8,2,160]{2,1,0:T(2,128)(2,1)}), bf16[8,2,160]{2,1,0:T(2,128)(2,1)S(1)}, u32[]{:S(2)}, u32[]{:S(2)}) async-start(bf16[8,2,160]{2,1,0:T(2,128)(2,1)} %reshape.399), calls=%async_computation.1 | async-start | bytes 16384 | tf_op jit(solution)/shard_map/all_to_all | solution.py:148
  20.5 32.2 %copy-start.32 = (f32[10]{0:T(128)}, f32[10]{0:T(128)S(1)}, u32[]{:S(2)}) copy-start(f32[10]{0:T(128)S(1)} %fusion.113) | copy-start | bytes 124
  25.1 28.4 %all-to-all-start = ((bf16[32,8,640]{2,0,1:T(8,128)(2,1)}), bf16[32,8,640]{2,0,1:T(8,128)(2,1)S(1)}, u32[]{:S(2)}, u32[]{:S(2)}) async-start(bf16[32,8,640]{2,0,1:T(8,128)(2,1)} %bitcast.236), calls=%async_computation | async-start | bytes 655360 | tf_op jit(solution)/shard_map/all_to_all | solution.py:147
  51.6 8.8 %copy-start.34 = (f32[10]{0:T(128)}, f32[10]{0:T(128)S(1)}, u32[]{:S(2)}) copy-start(f32[10]{0:T(128)S(1)} %dynamic_slice.73) | copy-start | bytes 124
  53.5 70.7 %copy-start.1 = (bf16[32,8,640]{2,0,1:T(8,128)(2,1)}, bf16[32,8,640]{2,0,1:T(8,128)(2,1)S(1)}, u32[]{:S(2)}) copy-start(bf16[32,8,640]{2,0,1:T(8,128)(2,1)S(1)} %all-to-all-done) | copy-start | bytes 983044
  53.5 20.2 %all-to-all-start.3 = ((bf16[32,8,640]{2,0,1:T(8,128)(2,1)}), bf16[32,8,640]{2,0,1:T(8,128)(2,1)S(1)}, u32[]{:S(2)}, u32[]{:S(2)}) async-start(bf16[32,8,640]{2,0,1:T(8,128)(2,1)} %bitcast.235), calls=%async_computation.3 | async-start | bytes 655360 | tf_op jit(solution)/shard_map/all_to_all | solution.py:149
  59.3 82.6 %all-gather.7.cloned.1.call-start = ((), (), s32[]{:S(2)}) async-start(), calls=%async_computation.7 | async-start | bytes 2785280 | tf_op jit(solution)/shard_map/all_gather | solution.py:13
  73.7 52.4 %copy-start.3 = (bf16[32,8,640]{2,0,1:T(8,128)(2,1)}, bf16[32,8,640]{2,0,1:T(8,128)(2,1)S(1)}, u32[]{:S(2)}) copy-start(bf16[32,8,640]{2,0,1:T(8,128)(2,1)S(1)} %all-to-all-done.3) | copy-start | bytes 983044
  83.0 123.3 %all-gather.9.cloned.1.call-start = ((), (), s32[]{:S(2)}) async-start(), calls=%async_computation.8 | async-start | bytes 5570560 | tf_op jit(solution)/shard_map/all_gather | solution.py:37
  266.0 8.9 %copy-start.36 = (f32[10]{0:T(128)}, f32[10]{0:T(128)S(1)}, u32[]{:S(2)}) copy-start(f32[10]{0:T(128)S(1)} %slice_bitcast_fusion) | copy-start | bytes 124
  304.5 17.2 %copy-start.7 = (bf16[32,2560]{1,0:T(8,128)(2,1)S(1)}, bf16[32,2560]{1,0:T(8,128)(2,1)}, u32[]{:S(2)}) copy-start(bf16[32,2560]{1,0:T(8,128)(2,1)} %param.12) | copy-start | bytes 491524
  308.2 13.3 %all-to-all-start.5 = ((bf16[8,2,160]{2,1,0:T(2,128)(2,1)}), bf16[8,2,160]{2,1,0:T(2,128)(2,1)S(1)}, u32[]{:S(2)}, u32[]{:S(2)}) async-start(bf16[8,2,160]{2,1,0:T(2,128)(2,1)} %reshape.401), calls=%async_computation.5 | async-start | bytes 16384 | tf_op jit(solution)/shard_map/all_to_all | solution.py:189
  314.9 31.9 %reduce-scatter.4.cloned.1.call-start = ((), (), s32[]{:S(2)}) async-start(), calls=%async_computation.9 | async-start | bytes 147456
  315.8 134.3 %all-reduce.8.cloned.1.call-start = ((), (), s32[]{:S(2)}) async-start(), calls=%async_computation.11 | async-start | bytes 6881280 | tf_op jit(solution)/shard_map/psum | solution.py:209
  349.5 100.5 %copy-start.39 = (f32[80]{0:T(128)S(1)}, f32[80]{0:T(128)}, u32[]{:S(2)}) copy-start(f32[80]{0:T(128)} %param.19) | copy-start | bytes 964
  349.6 101.0 %copy-start.11 = (f32[256,10]{1,0:T(8,128)S(1)}, f32[256,10]{1,0:T(8,128)}, u32[]{:S(2)}) copy-start(f32[256,10]{1,0:T(8,128)} %copy-done.10) | copy-start | bytes 30724
  349.6 210.2 %all-reduce.6.cloned.1.call-start = ((), (), s32[]{:S(2)}) async-start(), calls=%async_computation.10 | async-start | bytes 6881280 | tf_op jit(solution)/shard_map/psum | solution.py:208
  469.5 69.2 %copy-start.26 = (bf16[32,256]{1,0:T(8,128)(2,1)S(1)}, bf16[32,256]{1,0:T(8,128)(2,1)}, u32[]{:S(2)}) copy-start(bf16[32,256]{1,0:T(8,128)(2,1)} %reduce-scatter.4.cloned.1.call-done) | copy-start | bytes 49156
  470.5 68.7 %copy-start.9 = (bf16[2560,80]{0,1:T(8,128)(2,1)S(1)}, bf16[2560,80]{0,1:T(8,128)(2,1)}, u32[]{:S(2)}) copy-start(bf16[2560,80]{0,1:T(8,128)(2,1)} %param.16) | copy-start | bytes 1228804
  470.5 15.4 %all-to-all-start.2 = ((bf16[8,32,640]{2,1,0:T(8,128)(2,1)}), bf16[8,32,640]{2,1,0:T(8,128)(2,1)S(1)}, u32[]{:S(2)}, u32[]{:S(2)}) async-start(bf16[8,32,640]{2,1,0:T(8,128)(2,1)} %get-tuple-element.548), calls=%async_computation.2 | async-start | bytes 655360 | tf_op jit(solution)/shard_map/all_to_all | solution.py:187
  485.9 54.9 %all-to-all-start.4 = ((bf16[8,32,640]{2,1,0:T(8,128)(2,1)}), bf16[8,32,640]{2,1,0:T(8,128)(2,1)S(1)}, u32[]{:S(2)}, u32[]{:S(2)}) async-start(bf16[8,32,640]{2,1,0:T(8,128)(2,1)} %get-tuple-element.547), calls=%async_computation.4 | async-start | bytes 655360 | tf_op jit(solution)/shard_map/all_to_all | solution.py:188
  (27 other events, 132.0 us)
Sparse Core Ops, SparseCore 0:
  83.1 58.7 all-gather.6
  144.9 61.3 all-gather.8
  318.8 27.9 reduce-scatter.3
  349.9 100.1 all-reduce.7
  453.4 106.2 all-reduce.5
